TPU v7x, 128 devices: a whole 4x4x4 slice. The times are simulated.
128 devices in a mesh: dyn: 64 (over x, y, z), grp: 2 (over core).
Axes of the slice: x: 4, y: 4, z: 4, core: 2. Of those that a mesh axis runs over, the one named last changes fastest.
Arguments:
- fields: float32 [16, 72, 32768], P(None, None, ('dyn', 'grp')), may hold values from -6 to 6
- velocity: float32 [2, 16, 72, 32768], P(None, None, None, ('dyn', 'grp')), may hold values from -1 to 1
- neighbors: int32 [4, 32768], P(None, ('dyn', 'grp')), may hold values from 0 to 32767, as said below
- column_slot: int32 [16, 32768], P(None, ('dyn', 'grp')), may hold values from 0 to 524287, as said below
- surface: bfloat16 [16, 524288], P(None, 'dyn'), may hold values from -6 to 6
- w_profile: bfloat16 [72, 1024], replicated, may hold values from -0.625 to 0.625
- w_surface: bfloat16 [16, 1024], replicated, may hold values from -0.625 to 0.625
- b_first: float32 [1024], replicated, may hold values from -4 to 4
- w_second: bfloat16 [1024, 1024], replicated, may hold values from -0.1875 to 0.1875
- b_second: float32 [1024], replicated, may hold values from -4 to 4
- w_third: bfloat16 [1024, 1024], replicated, may hold values from -0.1875 to 0.1875
- b_third: float32 [1024], replicated, may hold values from -4 to 4
- w_out: bfloat16 [1024, 72], replicated, may hold values from -0.1875 to 0.1875
- b_out: float32 [72], replicated, may hold values from -3 to 3
Outputs:
- advanced_state: float32 [16, 72, 32768], P(None, None, ('dyn', 'grp'))
- heating: bfloat16 [16, 72, 32768], P(None, None, ('dyn', 'grp'))
Inputs may be any that keep to these rules, and one draw needn't show every extreme that they name: neighbors[k, e] = (e + o) mod 32768 with 1 <= |o| <= 32; |o| = 32 occurs. `column_slot`: all slots are distinct. With e // 256 = 2 d + g, every column (n, e) gets slot b * 2 * 4096 + g * 4096 + d * 64 + k with 0 <= k < 64; each pair of source and block b gets exactly 64 columns.
All inputs are finite; a program needn't handle non-finite values.
Results may differ from a plain program's by a relative error of at most 0.0053.
Values may be sent and summed in bfloat16 or wider, within the bound.
No kernel may reach another device: no remote copies, remote signals or barrier semaphores. Data moves between devices by JAX's collectives and lax.ppermute only.
A program may use at most 192 MiB of HBM per device.

v0:
```python
import functools
import math

import jax
import jax.numpy as jnp
import numpy as np
from jax import lax
from jax.experimental import pallas as pl
from jax.experimental.pallas import tpu as pltpu
from jax.sharding import PartitionSpec as P

NODES = 16
LEV = 72
STEPS = 4
LANES = 128
STEP_SIZE = 0.05
LIFT = 6.0
EDGES = ((0, 1, 2, 3), (12, 13, 14, 15), (0, 4, 8, 12), (3, 7, 11, 15))
OPPOSITE = (1, 0, 3, 2)
NET_LIMIT = 117 << 19
ADVANCE_LIMIT = 36 << 20
HALO_ROWS = 3 * NODES * LEV + 16
BF16 = jnp.bfloat16
F32 = jnp.float32


def gll_derivative():
    points = np.array([-1.0, -math.sqrt(0.2), math.sqrt(0.2), 1.0])
    table = np.zeros((4, 4))
    for i in range(4):
        for m in range(4):
            if i == m:
                table[i, m] = sum(1.0 / (points[i] - points[r]) for r in range(4) if r != i)
            else:
                upper, lower = 1.0, 1.0
                for r in range(4):
                    if r != i and r != m:
                        upper = upper * (points[i] - points[r])
                    if r != m:
                        lower = lower * (points[m] - points[r])
                table[i, m] = upper / lower
    return table


DERIV = gll_derivative()


def low_half(rows):
    return lax.broadcasted_iota(jnp.int32, (rows, LANES), 1) < 64


def pack_surface(surface_ref, out_ref, token_ref, columns_ref, sems):
    token_ref[...] = jnp.zeros((8, LANES), F32)
    cols_dev = columns_ref.shape[1]
    start = pl.multiple_of(lax.axis_index("grp") * cols_dev, cols_dev)
    chunk = cols_dev // 4
    copies = []
    for part in range(4):
        copies.append(
            pltpu.make_async_copy(
                surface_ref.at[:, pl.ds(start + chunk * part, chunk)],
                columns_ref.at[:, chunk * part : chunk * part + chunk],
                sems.at[part],
            )
        )
        copies[-1].start()
    low = low_half(8)
    for part in range(4):
        copies[part].wait()
        for pair in range(chunk // LANES * part, chunk // LANES * (part + 1)):
            tile = columns_ref[:, LANES * pair : LANES * pair + LANES].astype(F32)
            upper, lower = tile[0:8], tile[8:16]
            out_ref[2 * pair] = jnp.where(low, upper, pltpu.roll(lower, 64, 1))
            out_ref[2 * pair + 1] = jnp.where(low, pltpu.roll(upper, 64, 1), lower)


def pack_halo(
    total,
    token_ref,
    fields_hbm,
    velocity_hbm,
    neighbors_hbm,
    near_ref,
    far_ref,
    fields_ref,
    velocity_ref,
    neighbors_ref,
    sems,
):
    del token_ref
    rows = NODES * LEV
    copies = [
        pltpu.make_async_copy(neighbors_hbm, neighbors_ref, sems.at[0]),
        pltpu.make_async_copy(fields_hbm, fields_ref, sems.at[1]),
        pltpu.make_async_copy(velocity_hbm.at[0], velocity_ref.at[0], sems.at[2]),
        pltpu.make_async_copy(velocity_hbm.at[1], velocity_ref.at[1], sems.at[3]),
    ]
    for copy in copies:
        copy.start()
    group = lax.axis_index("grp")
    first = (2 * lax.axis_index("dyn") + group) * fields_ref.shape[2]

    def fill(pairs):
        copies[0].wait()
        for out_ref, tile in pairs:
            lanes = slice(LANES * tile, LANES * tile + LANES)
            element = first + LANES * tile + lax.broadcasted_iota(jnp.int32, (4, LANES), 1)
            distance = neighbors_ref[:, lanes] - element
            distance = ((distance + total // 2) & (total - 1)) - total // 2
            padded = jnp.concatenate([distance.astype(F32), jnp.zeros((12, LANES), F32)], axis=0)
            out_ref[3 * rows : HALO_ROWS, :] = padded.astype(BF16)
        copies[1].wait()
        for out_ref, tile in pairs:
            lanes = slice(LANES * tile, LANES * tile + LANES)
            out_ref[0:rows, :] = fields_ref[:, :, lanes].reshape(rows, LANES).astype(BF16)
        for wind in range(2):
            copies[2 + wind].wait()
            for out_ref, tile in pairs:
                lanes = slice(LANES * tile, LANES * tile + LANES)
                out_ref[rows * (1 + wind) : rows * (2 + wind), :] = (
                    velocity_ref[wind, :, :, lanes].reshape(rows, LANES).astype(BF16)
                )

    @pl.when(group == 0)
    def _():
        fill([(far_ref, 0), (near_ref, 1)])

    @pl.when(group != 0)
    def _():
        fill([(far_ref, 1), (near_ref, 0)])


def silu_half(half):
    return (half + half * jnp.tanh(half)).astype(BF16)


def column_network(*refs):
    arrived_ref = refs[0]
    operands = refs[1:12]
    out_ref = refs[12]
    (
        w_profile_ref,
        w_surface_ref,
        slot_ref,
        fields_ref,
        b_first_ref,
        w_second_ref,
        b_second_ref,
        w_third_ref,
        b_third_ref,
        w_out_ref,
        b_out_ref,
    ) = refs[13:24]
    table_ref, input_ref, w_first_ref, sems = refs[24:]
    copies = [
        pltpu.make_async_copy(source, target, sems.at[i])
        for i, (source, target) in enumerate(zip(operands, refs[13:24]))
    ]
    for copy in copies:
        copy.start()
    low = low_half(8)
    for high in range(16):
        a, b, c, d = [arrived_ref[4 * high + r] for r in range(4)]
        upper = [jnp.where(low, a, pltpu.roll(b, 64, 1)), jnp.where(low, c, pltpu.roll(d, 64, 1))]
        lower = [jnp.where(low, pltpu.roll(a, 64, 1), b), jnp.where(low, pltpu.roll(c, 64, 1), d)]
        tile = jnp.concatenate(
            [jnp.concatenate(upper, axis=1), jnp.concatenate(lower, axis=1)], axis=0
        )
        table_ref[16 * high : 16 * high + 16, :] = tile.astype(BF16)
    copies[0].wait()
    copies[1].wait()
    hidden = w_first_ref.shape[1]
    w_first_ref[...] = jnp.concatenate(
        [
            w_profile_ref[...].astype(F32),
            w_surface_ref[...].astype(F32),
            jnp.zeros((8, hidden), F32),
        ],
        axis=0,
    ).astype(BF16)

    def prepare(node, place):
        slot = slot_ref[pl.ds(node, 1), :]
        placed = (slot >> 13) * 64 + (slot & 63)
        within = placed & 255
        high = placed >> 8
        rows = lax.broadcasted_iota(jnp.int32, (256, 256), 0)
        chosen = jnp.where(rows == within, 1.0, 0.0).astype(BF16)
        spread = jnp.dot(table_ref[...], chosen, preferred_element_type=F32)
        total = jnp.zeros((16, 256), F32)
        for h in range(16):
            total = total + jnp.where(high == h, spread[16 * h : 16 * h + 16, :], 0.0)
        column = jnp.concatenate([fields_ref[node], total, jnp.zeros((8, 256), F32)], axis=0)
        input_ref[place, 256 * (node % 4) : 256 * (node % 4) + 256, :] = (
            jnp.transpose(column).astype(BF16) * BF16(0.5)
        )

    def layer(value, w_ref, b_ref):
        return silu_half(
            jnp.dot(value, w_ref[...], preferred_element_type=F32) + 0.5 * b_ref[...]
        )

    for copy in copies[2:5]:
        copy.wait()
    for j in range(4):
        prepare(j, 0)
    for block in range(4):
        def ahead(j):
            if block < 3:
                prepare(4 * block + 4 + j, (block + 1) % 2)

        value = layer(input_ref[block % 2], w_first_ref, b_first_ref) * BF16(0.5)
        if block == 0:
            copies[5].wait()
            copies[6].wait()
        ahead(0)
        ahead(1)
        value = layer(value, w_second_ref, b_second_ref) * BF16(0.5)
        if block == 0:
            for copy in copies[7:11]:
                copy.wait()
            diagonal = lax.broadcasted_iota(jnp.int32, (LEV, LEV), 0) == lax.broadcasted_iota(
                jnp.int32, (LEV, LEV), 1
            )
            b_out = jnp.sum(jnp.where(diagonal, b_out_ref[...], 0.0), axis=1, keepdims=True)
        ahead(2)
        ahead(3)
        value = layer(value, w_third_ref, b_third_ref)
        result = lax.dot_general(
            w_out_ref[...], value, (((1,), (1,)), ((), ())), preferred_element_type=F32
        )
        result = result + b_out
        for j in range(4):
            out_ref[4 * block + j] = result[:, 256 * j : 256 * j + 256].astype(BF16)


class Dynamics:
    def __init__(self, total, refs):
        (
            self.current,
            self.velocity,
            self.neighbors,
            self.near,
            self.far,
            self.wind,
            self.chosen,
            self.across,
        ) = refs
        self.total = total

    def mix(self, start, count):
        low = low_half(count)
        group = lax.axis_index("grp")
        mask = jnp.logical_xor(low, jnp.broadcast_to(group, (count, LANES)) != 0)
        near = self.near[start : start + count, :].astype(F32)
        far = self.far[start : start + count, :].astype(F32)
        return jnp.where(mask, near, far), jnp.where(mask, far, near)

    def spread(self):
        rows = NODES * LEV
        for pair in range(8):
            nodes = slice(2 * pair, 2 * pair + 2)
            inner, outer = self.mix(144 * pair, 144)
            self.current[nodes, :, 256:384] = inner.reshape(2, LEV, LANES)
            self.current[nodes, :, 384:512] = outer.reshape(2, LEV, LANES)
            for w in range(2):
                inner, outer = self.mix(rows * (1 + w) + 144 * pair, 144)
                self.wind[w, nodes, :, 0:128] = inner.reshape(2, LEV, LANES)
                self.wind[w, nodes, :, 128:256] = outer.reshape(2, LEV, LANES)

    def choose(self):
        total = self.total
        first = (2 * lax.axis_index("dyn") + lax.axis_index("grp")) * 256
        inner, outer = self.mix(3 * NODES * LEV, 16)
        lane = lax.broadcasted_iota(jnp.int32, (4, LANES), 1)
        right = lane + 256
        left = lane - 128
        own = self.neighbors[...] - first
        own = ((own + total // 2) & (total - 1)) - total // 2
        place = jnp.concatenate(
            [
                own,
                jnp.where(lane < 64, right, left) + inner[0:4].astype(jnp.int32),
                jnp.where(lane < 64, left, right) + outer[0:4].astype(jnp.int32),
            ],
            axis=1,
        )
        place = jnp.where(
            place < -64,
            place + 512,
            jnp.where(place < 0, place + 384, jnp.where(place >= 320, place + 128, place)),
        )
        source = lax.broadcasted_iota(jnp.int32, (512, 512), 0)
        for k in range(4):
            self.chosen[k] = jnp.where(source == place[k : k + 1, :], 1.0, 0.0).astype(BF16)

    def move(self, tiles_in, tiles_out):
        width_in, width_out = LANES * tiles_in, LANES * tiles_out
        for k in range(4):
            facing = jnp.concatenate(
                [self.current[n, :, 0:width_in] for n in EDGES[OPPOSITE[k]]], axis=0
            ).astype(BF16)
            moved = jnp.dot(
                facing, self.chosen[k, 0:width_in, 0:width_out], preferred_element_type=F32
            )
            self.across[k, :, :, 0:width_out] = moved.reshape(4, LEV, width_out)

    def update(self, tiles_out):
        table = STEP_SIZE * DERIV
        gain = STEP_SIZE * LIFT

        def levels(part):
            for t in range(tiles_out):
                lanes = slice(LANES * t, LANES * t + LANES)
                value = [self.current[n, part, lanes] for n in range(NODES)]
                for n in range(NODES):
                    i, j = n // 4, n % 4
                    if t < 2:
                        winds = [self.velocity[w, n, part, lanes] for w in range(2)]
                    else:
                        shifted = slice(LANES * (t - 2), LANES * (t - 1))
                        winds = [self.wind[w, n, part, shifted] for w in range(2)]
                    along = [
                        [(table[i, m], value[4 * m + j]) for m in range(4)],
                        [(table[j, m], value[4 * i + m]) for m in range(4)],
                    ]
                    slopes = []
                    for terms in along:
                        kept = [float(f) * v for f, v in terms if abs(f) > 1e-12]
                        slopes.append(functools.reduce(lambda p, q: p + q, kept))
                    sides = [
                        self.across[k, EDGES[k].index(n), part, lanes]
                        for k in range(4)
                        if n in EDGES[k]
                    ]
                    new = value[n] - (winds[0] * slopes[0] + winds[1] * slopes[1])
                    if sides:
                        gathered = functools.reduce(lambda p, q: p + q, sides)
                        new = new + gain * (gathered - float(len(sides)) * value[n])
                    self.current[n, part, lanes] = new

        for index in range(LEV // 8):
            levels(slice(8 * index, 8 * index + 8))


def advance(
    total,
    fields_hbm,
    velocity_hbm,
    neighbors_hbm,
    near_ref,
    far_ref,
    heating_hbm,
    out_ref,
    current_ref,
    velocity_ref,
    neighbors_ref,
    wind_ref,
    chosen_ref,
    across_ref,
    heating_ref,
    sems,
):
    copies = [
        pltpu.make_async_copy(neighbors_hbm, neighbors_ref, sems.at[0]),
        pltpu.make_async_copy(fields_hbm, current_ref.at[:, :, 0:256], sems.at[1]),
        pltpu.make_async_copy(velocity_hbm, velocity_ref, sems.at[2]),
        pltpu.make_async_copy(heating_hbm, heating_ref, sems.at[3]),
    ]
    for copy in copies:
        copy.start()
    dynamics = Dynamics(
        total,
        (
            current_ref,
            velocity_ref,
            neighbors_ref,
            near_ref,
            far_ref,
            wind_ref,
            chosen_ref,
            across_ref,
        ),
    )
    copies[0].wait()
    dynamics.choose()
    dynamics.spread()
    copies[1].wait()
    for tiles_in, tiles_out in ((4, 4), (4, 3), (3, 3), (3, 2)):
        dynamics.move(tiles_in, tiles_out)
        if tiles_in == 4 and tiles_out == 4:
            copies[2].wait()
        dynamics.update(tiles_out)
    copies[3].wait()
    for n in range(NODES):
        out_ref[n] = current_ref[n, :, 0:256] + heating_ref[n].astype(F32)


def per_device(
    fields,
    velocity,
    neighbors,
    column_slot,
    surface,
    w_profile,
    w_surface,
    b_first,
    w_second,
    b_second,
    w_third,
    b_third,
    w_out,
    b_out,
):
    elem_dev = fields.shape[2]
    devices = lax.axis_size(("dyn", "grp"))
    chips = lax.axis_size("dyn")
    total = elem_dev * devices
    vmem = pl.BlockSpec(memory_space=pltpu.VMEM)
    hbm = pl.BlockSpec(memory_space=pl.ANY)
    cols_dev = NODES * elem_dev
    packed, token = pl.pallas_call(
        pack_surface,
        out_shape=[
            jax.ShapeDtypeStruct((chips, 8, LANES), F32),
            jax.ShapeDtypeStruct((8, LANES), F32),
        ],
        in_specs=[hbm],
        out_specs=[vmem, vmem],
        scratch_shapes=[pltpu.VMEM((16, cols_dev), BF16), pltpu.SemaphoreType.DMA((4,))],
        name="pack_surface",
    )(surface)
    arrived = lax.all_to_all(packed, "dyn", split_axis=0, concat_axis=0, tiled=True)
    near, far = pl.pallas_call(
        functools.partial(pack_halo, total),
        out_shape=[jax.ShapeDtypeStruct((HALO_ROWS, LANES), BF16)] * 2,
        in_specs=[hbm] * 4,
        out_specs=[vmem, vmem],
        scratch_shapes=[
            pltpu.VMEM(fields.shape, F32),
            pltpu.VMEM(velocity.shape, F32),
            pltpu.VMEM(neighbors.shape, jnp.int32),
            pltpu.SemaphoreType.DMA((4,)),
        ],
        compiler_params=pltpu.CompilerParams(vmem_limit_bytes=58 << 20),
        cost_estimate=pl.CostEstimate(flops=10**6, bytes_accessed=7 * 10**6, transcendentals=0),
        name="pack_halo",
    )(token, fields, velocity, neighbors)
    near = lax.ppermute(near, ("dyn", "grp"), [(i, i ^ 1) for i in range(devices)])
    far = lax.ppermute(
        far, ("dyn", "grp"), [(i, (((i + 1) ^ 1) - 1) % devices) for i in range(devices)]
    )
    operands = [
        w_profile,
        w_surface,
        column_slot,
        fields,
        b_first[None, :],
        w_second,
        b_second[None, :],
        w_third,
        b_third[None, :],
        jnp.transpose(w_out),
        b_out[None, :],
    ]
    heating = pl.pallas_call(
        column_network,
        out_shape=jax.ShapeDtypeStruct((NODES, LEV, elem_dev), BF16),
        in_specs=[vmem] + [hbm] * len(operands),
        out_specs=vmem,
        scratch_shapes=[pltpu.VMEM(x.shape, x.dtype) for x in operands]
        + [
            pltpu.VMEM((256, 256), BF16),
            pltpu.VMEM((2, 1024, 96), BF16),
            pltpu.VMEM((96, w_second.shape[0]), BF16),
            pltpu.SemaphoreType.DMA((len(operands),)),
        ],
        compiler_params=pltpu.CompilerParams(vmem_limit_bytes=NET_LIMIT),
        cost_estimate=pl.CostEstimate(
            flops=22 * 10**9, bytes_accessed=8 * 10**6, transcendentals=12 * 10**6
        ),
        name="column_network",
    )(arrived, *operands)
    advanced = pl.pallas_call(
        functools.partial(advance, total),
        out_shape=jax.ShapeDtypeStruct((NODES, LEV, elem_dev), F32),
        in_specs=[hbm, hbm, hbm, vmem, vmem, hbm],
        out_specs=vmem,
        scratch_shapes=[
            pltpu.VMEM((NODES, LEV, 512), F32),
            pltpu.VMEM(velocity.shape, F32),
            pltpu.VMEM(neighbors.shape, jnp.int32),
            pltpu.VMEM((2, NODES, LEV, 256), F32),
            pltpu.VMEM((4, 512, 512), BF16),
            pltpu.VMEM((4, 4, LEV, 512), F32),
            pltpu.VMEM((NODES, LEV, elem_dev), BF16),
            pltpu.SemaphoreType.DMA((4,)),
        ],
        compiler_params=pltpu.CompilerParams(vmem_limit_bytes=ADVANCE_LIMIT),
        cost_estimate=pl.CostEstimate(
            flops=2 * 10**9, bytes_accessed=10 * 10**6, transcendentals=0
        ),
        name="advance",
    )(fields, velocity, neighbors, near, far, heating)
    return (advanced, heating)


def solution(mesh):
    sharded = ("dyn", "grp")
    in_specs = (
        P(None, None, sharded),
        P(None, None, None, sharded),
        P(None, sharded),
        P(None, sharded),
        P(None, "dyn"),
    ) + (P(),) * 9
    out_specs = (P(None, None, sharded), P(None, None, sharded))
    return jax.shard_map(
        per_device, mesh=mesh, in_specs=in_specs, out_specs=out_specs, check_vma=False
    )
```

profile of v0, /device:TPU:0, one launch (start us, length us, event | category | flops | bytes accessed | tf_op | source)
XLA Modules:
  0.0 62.8 jit_solution(4457768315916412251)
XLA Ops:
  0.6 1.8 %pack_surface.1 = (f32[64,8,128]{2,1,0:T(8,128)}, f32[8,128]{1,0:T(8,128)}) custom-call(bf16[16,8192]{1,0:T(8,128)(2,1)} %surface_ref.1), custom_call_target="tpu_custom_call" | custom-call | tf_op jit(solution)/shard_map/pack_surface/pallas_call | solution.py:422
  2.5 11.5 %all-to-all-start = ((f32[64,8,128]{2,1,0:T(8,128)}), f32[64,8,128]{2,1,0:T(8,128)S(1)}, u32[]{:S(2)}, u32[]{:S(2)}) async-start(f32[64,8,128]{2,1,0:T(8,128)} %get-tuple-element.9), calls=%async_computation | async-start | bytes 524288 | tf_op jit(solution)/shard_map/all_to_all | solution.py:433
  14.0 3.3 %pack_halo.1 = (bf16[3472,128]{1,0:T(8,128)(2,1)}, bf16[3472,128]{1,0:T(8,128)(2,1)}) custom-call(f32[8,128]{1,0:T(8,128)} %get-tuple-element.6.token_ref, f32[16,72,256]{2,1,0:T(8,128)} %fields_hbm.3, f32[2,16,72,256]{3,2,1,0:T(8,128)} %velocity_hbm.3, s32[4,256]{1,0:T(4,128)} %neighbors_hbm.3), custom_call_target="tpu_custom_call" | custom-call | flops 1000000 | bytes 7000000 | tf_op jit(solution)/shard_map/pack_halo/pallas_call | solution.py:434
  17.3 0.1 collective-permute-start
  17.4 7.4 %collective-permute-start.1 = (bf16[3472,128]{1,0:T(8,128)(2,1)}, bf16[3472,128]{1,0:T(8,128)(2,1)S(1)}, u32[]{:S(2)}, u32[]{:S(2)}) collective-permute-start(bf16[3472,128]{1,0:T(8,128)(2,1)} %get-tuple-element.8), channel_id=1, source_target_pairs={{0,127},{1,2},{2,1},{3,4},{4,3},{5,6},{6,5},{7,8},{8,7},{9,10},{10... | collective-permute-start | bytes 2666504 | tf_op jit(solution)/shard_map/ppermute | solution.py:450
  24.8 0.0 all-to-all-done.refs_0_
  24.8 0.0 copy-start.4
  24.8 0.7 %copy-done.4 = f32[64,8,128]{2,1,0:T(8,128)} copy-done((f32[64,8,128]{2,1,0:T(8,128)}, f32[64,8,128]{2,1,0:T(8,128)S(1)}, u32[]{:S(2)}) %copy-start.4) | copy-done | bytes 262168
  25.6 0.0 copy-start
  25.6 0.0 copy-start.1
  25.6 0.0 copy-start.2
  25.6 27.6 %column_network.1.heating_hbm = bf16[16,72,256]{2,1,0:T(8,128)(2,1)} custom-call(f32[64,8,128]{2,1,0:T(8,128)} %copy-done.4, bf16[72,1024]{1,0:T(8,128)(2,1)} %refs_1_.1, bf16[16,1024]{1,0:T(8,128)(2,1)} %refs_2_.1, s32[16,256]{1,0:T(8,128)} %refs_3_.1, f32[16,72,256]{2,1,0:T(8,128)} %fields_hbm.3, f32[1,1024]{1,0:T(1,128)} %bitcast.6, ...), custom_call_target="tpu_custom_call" | custom-call | flops 22000001024 | bytes 8000000 | tf_op jit(solution)/shard_map/column_network/pallas_call | solution.py:466
  53.2 0.0 collective-permute-done.near_ref
  53.2 0.0 collective-permute-done.1.far_ref
  53.2 0.0 copy-done
  53.2 0.0 copy-done.1
  53.2 0.0 copy-done.2
  53.2 0.0 copy-start.3
  53.2 1.1 %copy-done.3 = bf16[16,72,256]{2,1,0:T(8,128)(2,1)S(1)} copy-done((bf16[16,72,256]{2,1,0:T(8,128)(2,1)S(1)}, bf16[16,72,256]{2,1,0:T(8,128)(2,1)}, u32[]{:S(2)}) %copy-start.3) | copy-done | bytes 589848
  54.3 8.3 %advance.1 = f32[16,72,256]{2,1,0:T(8,128)} custom-call(f32[16,72,256]{2,1,0:T(8,128)S(1)} %copy-done.1, f32[2,16,72,256]{3,2,1,0:T(8,128)S(1)} %copy-done, s32[4,256]{1,0:T(4,128)S(1)} %copy-done.2, bf16[3472,128]{1,0:T(8,128)(2,1)S(1)} %collective-permute-done.near_ref, bf16[3472,128]{1,0:T(8,128)(2,1)S(1)} %collective-permute-done.1.far_ref, ...), custom_call_target="tpu_custom_call" | custom-call | flops 2000000000 | bytes 10000000 | tf_op jit(solution)/shard_map/advance/pallas_call | solution.py:484
Async XLA Ops:
  2.5 22.4 %all-to-all-start = ((f32[64,8,128]{2,1,0:T(8,128)}), f32[64,8,128]{2,1,0:T(8,128)S(1)}, u32[]{:S(2)}, u32[]{:S(2)}) async-start(f32[64,8,128]{2,1,0:T(8,128)} %get-tuple-element.9), calls=%async_computation | async-start | bytes 524288 | tf_op jit(solution)/shard_map/all_to_all | solution.py:433
  17.3 35.9 %collective-permute-start = (bf16[3472,128]{1,0:T(8,128)(2,1)}, bf16[3472,128]{1,0:T(8,128)(2,1)S(1)}, u32[]{:S(2)}, u32[]{:S(2)}) collective-permute-start(bf16[3472,128]{1,0:T(8,128)(2,1)} %get-tuple-element.7), channel_id=1, source_target_pairs={{0,1},{1,0},{2,3},{3,2},{4,5},{5,4},{6,7},{7,6},{8,9},{9,8},{10,11... | collective-permute-start | bytes 2666504 | tf_op jit(solution)/shard_map/ppermute | solution.py:449
  17.4 35.8 %collective-permute-start.1 = (bf16[3472,128]{1,0:T(8,128)(2,1)}, bf16[3472,128]{1,0:T(8,128)(2,1)S(1)}, u32[]{:S(2)}, u32[]{:S(2)}) collective-permute-start(bf16[3472,128]{1,0:T(8,128)(2,1)} %get-tuple-element.8), channel_id=1, source_target_pairs={{0,127},{1,2},{2,1},{3,4},{4,3},{5,6},{6,5},{7,8},{8,7},{9,10},{10... | collective-permute-start | bytes 2666504 | tf_op jit(solution)/shard_map/ppermute | solution.py:450
  24.8 0.7 %copy-start.4 = (f32[64,8,128]{2,1,0:T(8,128)}, f32[64,8,128]{2,1,0:T(8,128)S(1)}, u32[]{:S(2)}) copy-start(f32[64,8,128]{2,1,0:T(8,128)S(1)} %all-to-all-done.refs_0_) | copy-start | bytes 786436
  25.6 27.7 %copy-start = (f32[2,16,72,256]{3,2,1,0:T(8,128)S(1)}, f32[2,16,72,256]{3,2,1,0:T(8,128)}, u32[]{:S(2)}) copy-start(f32[2,16,72,256]{3,2,1,0:T(8,128)} %velocity_hbm.3) | copy-start | bytes 7077892
  25.6 27.7 %copy-start.1 = (f32[16,72,256]{2,1,0:T(8,128)S(1)}, f32[16,72,256]{2,1,0:T(8,128)}, u32[]{:S(2)}) copy-start(f32[16,72,256]{2,1,0:T(8,128)} %fields_hbm.3) | copy-start | bytes 3538948
  25.6 27.7 %copy-start.2 = (s32[4,256]{1,0:T(4,128)S(1)}, s32[4,256]{1,0:T(4,128)}, u32[]{:S(2)}) copy-start(s32[4,256]{1,0:T(4,128)} %neighbors_hbm.3) | copy-start | bytes 12292
  53.2 1.1 %copy-start.3 = (bf16[16,72,256]{2,1,0:T(8,128)(2,1)S(1)}, bf16[16,72,256]{2,1,0:T(8,128)(2,1)}, u32[]{:S(2)}) copy-start(bf16[16,72,256]{2,1,0:T(8,128)(2,1)} %column_network.1.heating_hbm) | copy-start | bytes 1769476
where the time goes:
time: 63.1 us; the launch traced here: 62.8 us
  Pallas kernels  41.1 us (65%)
  starting transfers between devices  19 us (30%)
  local copies, waits for them, and re-layouts  1.79 us (3%)
  between operations  0.9 us (1%)
    pallas_call x1, Pallas kernels, per_device(): pl.pallas_call(column_network, out_shape=jax.ShapeDtypeStruct((NODES, LEV...  27.6 us
    all_to_all x1, starting transfers between devices, per_device(): lax.all_to_all(packed, 'dyn', split_axis=0, concat_axis=0, tiled=True)  11.5 us
    pallas_call x1, Pallas kernels, per_device(): pl.pallas_call(functools.partial(advance, total), out_shape=jax.ShapeDtyp...  8.29 us
    ppermute x1, starting transfers between devices, per_device(): lax.ppermute(far, ('dyn', 'grp'), [(i, ((i + 1 ^ 1) - 1) % devices) for i...  7.41 us
    pallas_call x1, Pallas kernels, per_device(): pl.pallas_call(functools.partial(pack_halo, total), out_shape=[jax.ShapeD...  3.33 us
    pallas_call x1, Pallas kernels, per_device(): pl.pallas_call(pack_surface, out_shape=[jax.ShapeDtypeStruct((chips, 8, L...  1.83 us
    unnamed x10, local copies, waits for them, and re-layouts  1.79 us
  transfers between devices with their start and end apart: 3, of which 0 were waited for; matrix products, arithmetic and copies ran while one was open for 0% of the time, Pallas kernels for 49%

commit v1 on v0

--- a/solution.py
+++ b/solution.py
@@ -53,25 +53,19 @@
     token_ref[...] = jnp.zeros((8, LANES), F32)
     cols_dev = columns_ref.shape[1]
     start = pl.multiple_of(lax.axis_index("grp") * cols_dev, cols_dev)
-    chunk = cols_dev // 4
-    copies = []
-    for part in range(4):
-        copies.append(
-            pltpu.make_async_copy(
-                surface_ref.at[:, pl.ds(start + chunk * part, chunk)],
-                columns_ref.at[:, chunk * part : chunk * part + chunk],
-                sems.at[part],
-            )
-        )
-        copies[-1].start()
+    copy = pltpu.make_async_copy(
+        surface_ref.at[:, pl.ds(start, cols_dev)], columns_ref, sems.at[0]
+    )
+    copy.start()
+    copy.wait()
     low = low_half(8)
-    for part in range(4):
-        copies[part].wait()
-        for pair in range(chunk // LANES * part, chunk // LANES * (part + 1)):
-            tile = columns_ref[:, LANES * pair : LANES * pair + LANES].astype(F32)
-            upper, lower = tile[0:8], tile[8:16]
-            out_ref[2 * pair] = jnp.where(low, upper, pltpu.roll(lower, 64, 1))
-            out_ref[2 * pair + 1] = jnp.where(low, pltpu.roll(upper, 64, 1), lower)
+    for pair in range(cols_dev // LANES):
+        tile = columns_ref[:, LANES * pair : LANES * pair + LANES].astype(F32)
+        upper, lower = tile[0:8], tile[8:16]
+        even = jnp.where(low, upper, pltpu.roll(lower, 64, 1))
+        odd = jnp.where(low, pltpu.roll(upper, 64, 1), lower)
+        out_ref[2 * pair] = even.astype(BF16)
+        out_ref[2 * pair + 1] = odd.astype(BF16)
 
 
 def pack_halo(
@@ -80,54 +74,83 @@
     fields_hbm,
     velocity_hbm,
     neighbors_hbm,
-    near_ref,
-    far_ref,
+    far_hbm,
+    near_hbm,
     fields_ref,
     velocity_ref,
     neighbors_ref,
+    far_ref,
+    near_ref,
     sems,
+    out_sems,
 ):
     del token_ref
     rows = NODES * LEV
-    copies = [
-        pltpu.make_async_copy(neighbors_hbm, neighbors_ref, sems.at[0]),
-        pltpu.make_async_copy(fields_hbm, fields_ref, sems.at[1]),
-        pltpu.make_async_copy(velocity_hbm.at[0], velocity_ref.at[0], sems.at[2]),
-        pltpu.make_async_copy(velocity_hbm.at[1], velocity_ref.at[1], sems.at[3]),
-    ]
+    half = NODES // 2
+    sources = [(fields_hbm, fields_ref)]
+    for wind in range(2):
+        sources.append((velocity_hbm.at[wind], velocity_ref.at[wind]))
+    copies = []
+    for array, (source, target) in enumerate(sources):
+        for part in range(2):
+            nodes = slice(half * part, half * part + half)
+            copies.append(
+                pltpu.make_async_copy(
+                    source.at[nodes], target.at[nodes], sems.at[2 * array + part]
+                )
+            )
+    neighbors_copy = pltpu.make_async_copy(neighbors_hbm, neighbors_ref, sems.at[6])
     for copy in copies:
         copy.start()
+    neighbors_copy.start()
     group = lax.axis_index("grp")
     first = (2 * lax.axis_index("dyn") + group) * fields_ref.shape[2]
 
-    def fill(pairs):
-        copies[0].wait()
-        for out_ref, tile in pairs:
-            lanes = slice(LANES * tile, LANES * tile + LANES)
-            element = first + LANES * tile + lax.broadcasted_iota(jnp.int32, (4, LANES), 1)
-            distance = neighbors_ref[:, lanes] - element
-            distance = ((distance + total // 2) & (total - 1)) - total // 2
-            padded = jnp.concatenate([distance.astype(F32), jnp.zeros((12, LANES), F32)], axis=0)
-            out_ref[3 * rows : HALO_ROWS, :] = padded.astype(BF16)
-        copies[1].wait()
-        for out_ref, tile in pairs:
-            lanes = slice(LANES * tile, LANES * tile + LANES)
-            out_ref[0:rows, :] = fields_ref[:, :, lanes].reshape(rows, LANES).astype(BF16)
-        for wind in range(2):
-            copies[2 + wind].wait()
+    def fill(far_tile):
+        sent = []
+
+        def send(start, count, number):
+            part = slice(start, start + count)
+            for side, (source, target) in enumerate(((far_ref, far_hbm), (near_ref, near_hbm))):
+                copy = pltpu.make_async_copy(
+                    source.at[part, :], target.at[part, :], out_sems.at[2 * number + side]
+                )
+                copy.start()
+                sent.append(copy)
+
+        pairs = [(far_ref, far_tile), (near_ref, 1 - far_tile)]
+        for number, copy in enumerate(copies):
+            copy.wait()
+            array, part = number // 2, number % 2
+            nodes = slice(half * part, half * part + half)
+            start, count = rows * array + half * LEV * part, half * LEV
             for out_ref, tile in pairs:
                 lanes = slice(LANES * tile, LANES * tile + LANES)
-                out_ref[rows * (1 + wind) : rows * (2 + wind), :] = (
-                    velocity_ref[wind, :, :, lanes].reshape(rows, LANES).astype(BF16)
-                )
+                value = sources[array][1][nodes, :, lanes]
+                out_ref[start : start + count, :] = value.reshape(count, LANES).astype(BF16)
+            if number == 5:
+                neighbors_copy.wait()
+                for out_ref, tile in pairs:
+                    lanes = slice(LANES * tile, LANES * tile + LANES)
+                    element = first + LANES * tile
+                    element = element + lax.broadcasted_iota(jnp.int32, (4, LANES), 1)
+                    distance = neighbors_ref[:, lanes] - element
+                    distance = ((distance + total // 2) & (total - 1)) - total // 2
+                    padded = [distance.astype(F32), jnp.zeros((12, LANES), F32)]
+                    padded = jnp.concatenate(padded, axis=0)
+                    out_ref[3 * rows : HALO_ROWS, :] = padded.astype(BF16)
+                count = count + HALO_ROWS - 3 * rows
+            send(start, count, number)
+        for copy in sent:
+            copy.wait()
 
     @pl.when(group == 0)
     def _():
-        fill([(far_ref, 0), (near_ref, 1)])
+        fill(0)
 
     @pl.when(group != 0)
     def _():
-        fill([(far_ref, 1), (near_ref, 0)])
+        fill(1)
 
 
 def silu_half(half):
@@ -135,10 +158,10 @@
 
 
 def column_network(*refs):
-    arrived_ref = refs[0]
-    operands = refs[1:12]
+    operands = refs[:12]
     out_ref = refs[12]
     (
+        arrived_ref,
         w_profile_ref,
         w_surface_ref,
         slot_ref,
@@ -150,25 +173,30 @@
         b_third_ref,
         w_out_ref,
         b_out_ref,
-    ) = refs[13:24]
-    table_ref, input_ref, w_first_ref, sems = refs[24:]
+    ) = refs[13:25]
+    table_ref, input_ref, w_first_ref, sems = refs[25:]
+    sources, targets = list(operands), list(refs[13:25])
+    sources[4], targets[4] = operands[4].at[0:4], fields_ref.at[0:4]
+    sources.append(operands[4].at[4:NODES])
+    targets.append(fields_ref.at[4:NODES])
     copies = [
         pltpu.make_async_copy(source, target, sems.at[i])
-        for i, (source, target) in enumerate(zip(operands, refs[13:24]))
+        for i, (source, target) in enumerate(zip(sources, targets))
     ]
     for copy in copies:
         copy.start()
+    copies[0].wait()
     low = low_half(8)
     for high in range(16):
-        a, b, c, d = [arrived_ref[4 * high + r] for r in range(4)]
+        a, b, c, d = [arrived_ref[4 * high + r].astype(F32) for r in range(4)]
         upper = [jnp.where(low, a, pltpu.roll(b, 64, 1)), jnp.where(low, c, pltpu.roll(d, 64, 1))]
         lower = [jnp.where(low, pltpu.roll(a, 64, 1), b), jnp.where(low, pltpu.roll(c, 64, 1), d)]
         tile = jnp.concatenate(
             [jnp.concatenate(upper, axis=1), jnp.concatenate(lower, axis=1)], axis=0
         )
         table_ref[16 * high : 16 * high + 16, :] = tile.astype(BF16)
-    copies[0].wait()
     copies[1].wait()
+    copies[2].wait()
     hidden = w_first_ref.shape[1]
     w_first_ref[...] = jnp.concatenate(
         [
@@ -200,7 +228,7 @@
             jnp.dot(value, w_ref[...], preferred_element_type=F32) + 0.5 * b_ref[...]
         )
 
-    for copy in copies[2:5]:
+    for copy in copies[3:5]:
         copy.wait()
     for j in range(4):
         prepare(j, 0)
@@ -209,15 +237,18 @@
             if block < 3:
                 prepare(4 * block + 4 + j, (block + 1) % 2)
 
+        if block == 0:
+            copies[5].wait()
         value = layer(input_ref[block % 2], w_first_ref, b_first_ref) * BF16(0.5)
         if block == 0:
-            copies[5].wait()
             copies[6].wait()
+            copies[7].wait()
+            copies[12].wait()
         ahead(0)
         ahead(1)
         value = layer(value, w_second_ref, b_second_ref) * BF16(0.5)
         if block == 0:
-            for copy in copies[7:11]:
+            for copy in copies[8:12]:
                 copy.wait()
             diagonal = lax.broadcasted_iota(jnp.int32, (LEV, LEV), 0) == lax.broadcasted_iota(
                 jnp.int32, (LEV, LEV), 1
@@ -305,39 +336,50 @@
             )
             self.across[k, :, :, 0:width_out] = moved.reshape(4, LEV, width_out)
 
+    def slopes(self, line):
+        table = STEP_SIZE * DERIV
+        sums = (line[0] + line[3], line[1] + line[2])
+        differences = (line[0] - line[3], line[1] - line[2])
+        out = [None] * 4
+        for i in range(2):
+            odd = [0.5 * float(table[i, m] - table[i, 3 - m]) for m in range(2)]
+            even = [0.5 * float(table[i, m] + table[i, 3 - m]) for m in range(2)]
+            p = odd[0] * differences[0] + odd[1] * differences[1]
+            q = even[0] * sums[0] + even[1] * sums[1]
+            out[i], out[3 - i] = p + q, p - q
+        return out
+
     def update(self, tiles_out):
-        table = STEP_SIZE * DERIV
         gain = STEP_SIZE * LIFT
 
         def levels(part):
             for t in range(tiles_out):
                 lanes = slice(LANES * t, LANES * t + LANES)
+                winds, shifted = self.velocity, lanes
+                if t >= 2:
+                    winds, shifted = self.wind, slice(LANES * (t - 2), LANES * (t - 1))
                 value = [self.current[n, part, lanes] for n in range(NODES)]
-                for n in range(NODES):
-                    i, j = n // 4, n % 4
-                    if t < 2:
-                        winds = [self.velocity[w, n, part, lanes] for w in range(2)]
-                    else:
-                        shifted = slice(LANES * (t - 2), LANES * (t - 1))
-                        winds = [self.wind[w, n, part, shifted] for w in range(2)]
-                    along = [
-                        [(table[i, m], value[4 * m + j]) for m in range(4)],
-                        [(table[j, m], value[4 * i + m]) for m in range(4)],
-                    ]
-                    slopes = []
-                    for terms in along:
-                        kept = [float(f) * v for f, v in terms if abs(f) > 1e-12]
-                        slopes.append(functools.reduce(lambda p, q: p + q, kept))
-                    sides = [
-                        self.across[k, EDGES[k].index(n), part, lanes]
-                        for k in range(4)
-                        if n in EDGES[k]
-                    ]
-                    new = value[n] - (winds[0] * slopes[0] + winds[1] * slopes[1])
-                    if sides:
-                        gathered = functools.reduce(lambda p, q: p + q, sides)
-                        new = new + gain * (gathered - float(len(sides)) * value[n])
-                    self.current[n, part, lanes] = new
+                new = [None] * NODES
+                for j in range(4):
+                    slopes = self.slopes([value[4 * i + j] for i in range(4)])
+                    for i in range(4):
+                        n = 4 * i + j
+                        sides = [
+                            self.across[k, EDGES[k].index(n), part, lanes]
+                            for k in range(4)
+                            if n in EDGES[k]
+                        ]
+                        new[n] = value[n] * (1.0 - gain * len(sides)) if sides else value[n]
+                        if sides:
+                            new[n] = new[n] + gain * functools.reduce(lambda p, q: p + q, sides)
+                        new[n] = new[n] - winds[0, n, part, shifted] * slopes[i]
+                for i in range(4):
+                    slopes = self.slopes(value[4 * i : 4 * i + 4])
+                    for j in range(4):
+                        n = 4 * i + j
+                        self.current[n, part, lanes] = (
+                            new[n] - winds[1, n, part, shifted] * slopes[j]
+                        )
 
         for index in range(LEV // 8):
             levels(slice(8 * index, 8 * index + 8))
@@ -348,10 +390,11 @@
     fields_hbm,
     velocity_hbm,
     neighbors_hbm,
+    far_ref,
     near_ref,
-    far_ref,
     heating_hbm,
     out_ref,
+    same_heating_hbm,
     current_ref,
     velocity_ref,
     neighbors_ref,
@@ -361,6 +404,7 @@
     heating_ref,
     sems,
 ):
+    del same_heating_hbm
     copies = [
         pltpu.make_async_copy(neighbors_hbm, neighbors_ref, sems.at[0]),
         pltpu.make_async_copy(fields_hbm, current_ref.at[:, :, 0:256], sems.at[1]),
@@ -422,27 +466,30 @@
     packed, token = pl.pallas_call(
         pack_surface,
         out_shape=[
-            jax.ShapeDtypeStruct((chips, 8, LANES), F32),
+            jax.ShapeDtypeStruct((chips, 8, LANES), BF16),
             jax.ShapeDtypeStruct((8, LANES), F32),
         ],
         in_specs=[hbm],
         out_specs=[vmem, vmem],
-        scratch_shapes=[pltpu.VMEM((16, cols_dev), BF16), pltpu.SemaphoreType.DMA((4,))],
+        scratch_shapes=[pltpu.VMEM((16, cols_dev), BF16), pltpu.SemaphoreType.DMA((1,))],
         name="pack_surface",
     )(surface)
     arrived = lax.all_to_all(packed, "dyn", split_axis=0, concat_axis=0, tiled=True)
-    near, far = pl.pallas_call(
+    far, near = pl.pallas_call(
         functools.partial(pack_halo, total),
         out_shape=[jax.ShapeDtypeStruct((HALO_ROWS, LANES), BF16)] * 2,
         in_specs=[hbm] * 4,
-        out_specs=[vmem, vmem],
+        out_specs=[hbm, hbm],
         scratch_shapes=[
             pltpu.VMEM(fields.shape, F32),
             pltpu.VMEM(velocity.shape, F32),
             pltpu.VMEM(neighbors.shape, jnp.int32),
-            pltpu.SemaphoreType.DMA((4,)),
+            pltpu.VMEM((HALO_ROWS, LANES), BF16),
+            pltpu.VMEM((HALO_ROWS, LANES), BF16),
+            pltpu.SemaphoreType.DMA((7,)),
+            pltpu.SemaphoreType.DMA((12,)),
         ],
-        compiler_params=pltpu.CompilerParams(vmem_limit_bytes=58 << 20),
+        compiler_params=pltpu.CompilerParams(vmem_limit_bytes=NET_LIMIT),
         cost_estimate=pl.CostEstimate(flops=10**6, bytes_accessed=7 * 10**6, transcendentals=0),
         name="pack_halo",
     )(token, fields, velocity, neighbors)
@@ -451,6 +498,7 @@
         far, ("dyn", "grp"), [(i, (((i + 1) ^ 1) - 1) % devices) for i in range(devices)]
     )
     operands = [
+        arrived,
         w_profile,
         w_surface,
         column_slot,
@@ -466,26 +514,30 @@
     heating = pl.pallas_call(
         column_network,
         out_shape=jax.ShapeDtypeStruct((NODES, LEV, elem_dev), BF16),
-        in_specs=[vmem] + [hbm] * len(operands),
+        in_specs=[hbm] * len(operands),
         out_specs=vmem,
         scratch_shapes=[pltpu.VMEM(x.shape, x.dtype) for x in operands]
         + [
             pltpu.VMEM((256, 256), BF16),
             pltpu.VMEM((2, 1024, 96), BF16),
             pltpu.VMEM((96, w_second.shape[0]), BF16),
-            pltpu.SemaphoreType.DMA((len(operands),)),
+            pltpu.SemaphoreType.DMA((len(operands) + 1,)),
         ],
         compiler_params=pltpu.CompilerParams(vmem_limit_bytes=NET_LIMIT),
         cost_estimate=pl.CostEstimate(
             flops=22 * 10**9, bytes_accessed=8 * 10**6, transcendentals=12 * 10**6
         ),
         name="column_network",
-    )(arrived, *operands)
-    advanced = pl.pallas_call(
+    )(*operands)
+    advanced, heating = pl.pallas_call(
         functools.partial(advance, total),
-        out_shape=jax.ShapeDtypeStruct((NODES, LEV, elem_dev), F32),
+        out_shape=[
+            jax.ShapeDtypeStruct((NODES, LEV, elem_dev), F32),
+            jax.ShapeDtypeStruct((NODES, LEV, elem_dev), BF16),
+        ],
+        input_output_aliases={5: 1},
         in_specs=[hbm, hbm, hbm, vmem, vmem, hbm],
-        out_specs=vmem,
+        out_specs=[vmem, hbm],
         scratch_shapes=[
             pltpu.VMEM((NODES, LEV, 512), F32),
             pltpu.VMEM(velocity.shape, F32),
@@ -501,7 +553,7 @@
             flops=2 * 10**9, bytes_accessed=10 * 10**6, transcendentals=0
         ),
         name="advance",
-    )(fields, velocity, neighbors, near, far, heating)
+    )(fields, velocity, neighbors, far, near, heating)
     return (advanced, heating)
 
 

time: 63.1 us -> 60.2 us (0.954); the launches traced: 62.8 us -> 59.2 us
  Pallas kernels: 41.1 us -> 39.3 us
  starting transfers between devices: 19 us -> 17.8 us
  local copies, waits for them, and re-layouts: 1.79 us -> 0.66 us
    ppermute x1, starting transfers between devices: 7.41 us -> 6.27 us  [per_device(): lax.ppermute(far, ('dyn', 'grp'), [(i, ((i + 1 ^ 1) - 1) % devices) for i...]
    unnamed x10 -> x8, local copies, waits for them, and re-layouts: 1.79 us -> 0.66 us
    pallas_call x1, Pallas kernels: 27.6 us -> 26.7 us  [per_device(): pl.pallas_call(column_network, out_shape=jax.ShapeDtypeStruct((NODES, LEV...]
  transfers between devices with their start and end apart: 3 -> 3, of which waited for: 0 -> 1; matrix products, arithmetic and copies ran while one was open for 0% -> 0% of each run, Pallas kernels for 49% -> 50%
where the time goes in v1:
time: 60.2 us; the launch traced here: 59.2 us
  Pallas kernels  39.3 us (65%)
  starting transfers between devices  17.8 us (30%)
  between operations  0.89 us (1%)
  local copies, waits for them, and re-layouts  0.66 us (1%)
  waiting for transfers between devices  0.62 us (1%)
    pallas_call x1, Pallas kernels, per_device(): pl.pallas_call(column_network, out_shape=jax.ShapeDtypeStruct((NODES, LEV...  26.7 us
    all_to_all x1, starting transfers between devices, per_device(): lax.all_to_all(packed, 'dyn', split_axis=0, concat_axis=0, tiled=True)  11.5 us
    pallas_call x1, Pallas kernels, per_device(): pl.pallas_call(functools.partial(advance, total), out_shape=[jax.ShapeDty...  7.99 us
    ppermute x1, starting transfers between devices, per_device(): lax.ppermute(far, ('dyn', 'grp'), [(i, ((i + 1 ^ 1) - 1) % devices) for i...  6.27 us
    pallas_call x1, Pallas kernels, per_device(): pl.pallas_call(functools.partial(pack_halo, total), out_shape=[jax.ShapeD...  2.89 us
    pallas_call x1, Pallas kernels, per_device(): pl.pallas_call(pack_surface, out_shape=[jax.ShapeDtypeStruct((chips, 8, L...  1.68 us
  transfers between devices with their start and end apart: 3, of which 1 were waited for; matrix products, arithmetic and copies ran while one was open for 0% of the time, Pallas kernels for 50%

profile of v1, /device:TPU:0, one launch (start us, length us, event | category | flops | bytes accessed | tf_op | source)
XLA Modules:
  0.0 59.2 jit_solution(444191402052494015)
XLA Ops:
  0.6 1.7 %pack_surface.1 = (bf16[64,8,128]{2,1,0:T(8,128)(2,1)}, f32[8,128]{1,0:T(8,128)}) custom-call(bf16[16,8192]{1,0:T(8,128)(2,1)} %surface_ref.1), custom_call_target="tpu_custom_call" | custom-call | tf_op jit(solution)/shard_map/pack_surface/pallas_call | solution.py:466
  2.3 11.5 %all-to-all-start = ((bf16[64,8,128]{2,1,0:T(8,128)(2,1)}), bf16[64,8,128]{2,1,0:T(8,128)(2,1)S(1)}, u32[]{:S(2)}, u32[]{:S(2)}) async-start(bf16[64,8,128]{2,1,0:T(8,128)(2,1)} %get-tuple-element.9), calls=%async_computation | async-start | bytes 262144 | tf_op jit(solution)/shard_map/all_to_all | solution.py:477
  13.8 2.9 %pack_halo.1 = (bf16[3472,128]{1,0:T(8,128)(2,1)}, bf16[3472,128]{1,0:T(8,128)(2,1)}) custom-call(f32[8,128]{1,0:T(8,128)} %get-tuple-element.6.token_ref, f32[16,72,256]{2,1,0:T(8,128)} %fields_hbm.3, f32[2,16,72,256]{3,2,1,0:T(8,128)} %velocity_hbm.3, s32[4,256]{1,0:T(4,128)} %neighbors_hbm.3), custom_call_target="tpu_custom_call" | custom-call | flops 1000000 | bytes 7000000 | tf_op jit(solution)/shard_map/pack_halo/pallas_call | solution.py:478
  16.7 6.3 %collective-permute-start = (bf16[3472,128]{1,0:T(8,128)(2,1)}, bf16[3472,128]{1,0:T(8,128)(2,1)S(1)}, u32[]{:S(2)}, u32[]{:S(2)}) collective-permute-start(bf16[3472,128]{1,0:T(8,128)(2,1)} %get-tuple-element.7), channel_id=1, source_target_pairs={{0,127},{1,2},{2,1},{3,4},{4,3},{5,6},{6,5},{7,8},{8,7},{9,10},{10... | collective-permute-start | bytes 2666504 | tf_op jit(solution)/shard_map/ppermute | solution.py:497
  23.0 0.0 collective-permute-start.1
  23.0 0.6 %all-to-all-done.refs_0_ = bf16[64,8,128]{2,1,0:T(8,128)(2,1)S(1)} async-done(((bf16[64,8,128]{2,1,0:T(8,128)(2,1)}), bf16[64,8,128]{2,1,0:T(8,128)(2,1)S(1)}, u32[]{:S(2)}, u32[]{:S(2)}) %all-to-all-start) | async-done | bytes 131104 | tf_op jit(solution)/shard_map/all_to_all | solution.py:477
  23.6 0.0 copy-start.3
  23.6 0.6 %copy-done.3 = bf16[64,8,128]{2,1,0:T(8,128)(2,1)} copy-done((bf16[64,8,128]{2,1,0:T(8,128)(2,1)}, bf16[64,8,128]{2,1,0:T(8,128)(2,1)S(1)}, u32[]{:S(2)}) %copy-start.3) | copy-done | bytes 131096
  24.3 0.0 copy-start
  24.3 0.0 copy-start.1
  24.3 0.0 copy-start.2
  24.3 26.7 %column_network.1.heating_hbm = bf16[16,72,256]{2,1,0:T(8,128)(2,1)} custom-call(bf16[64,8,128]{2,1,0:T(8,128)(2,1)} %copy-done.3, bf16[72,1024]{1,0:T(8,128)(2,1)} %refs_1_.1, bf16[16,1024]{1,0:T(8,128)(2,1)} %refs_2_.1, s32[16,256]{1,0:T(8,128)} %refs_3_.1, f32[16,72,256]{2,1,0:T(8,128)} %fields_hbm.3, f32[1,1024]{1,0:T(1,128)} %bitcast.6, ...), custom_call_target="tpu_custom_call" | custom-call | flops 22000001024 | bytes 8000000 | tf_op jit(solution)/shard_map/column_network/pallas_call | solution.py:514
  51.0 0.0 collective-permute-done.far_ref
  51.0 0.0 collective-permute-done.1.near_ref
  51.0 0.0 copy-done
  51.0 0.0 copy-done.1
  51.0 0.0 copy-done.2
  51.0 8.0 %advance.1 = (f32[16,72,256]{2,1,0:T(8,128)}, bf16[16,72,256]{2,1,0:T(8,128)(2,1)}) custom-call(f32[16,72,256]{2,1,0:T(8,128)S(1)} %copy-done.1, f32[2,16,72,256]{3,2,1,0:T(8,128)S(1)} %copy-done, s32[4,256]{1,0:T(4,128)S(1)} %copy-done.2, bf16[3472,128]{1,0:T(8,128)(2,1)S(1)} %collective-permute-done.far_ref, ...), custom_call_target="tpu_custom_call", output_to_operand_aliasing={{1}: (5, {})} | custom-call | flops 2000000000 | bytes 10000000 | tf_op jit(solution)/shard_map/advance/pallas_call | solution.py:532
Async XLA Ops:
  2.3 21.3 %all-to-all-start = ((bf16[64,8,128]{2,1,0:T(8,128)(2,1)}), bf16[64,8,128]{2,1,0:T(8,128)(2,1)S(1)}, u32[]{:S(2)}, u32[]{:S(2)}) async-start(bf16[64,8,128]{2,1,0:T(8,128)(2,1)} %get-tuple-element.9), calls=%async_computation | async-start | bytes 262144 | tf_op jit(solution)/shard_map/all_to_all | solution.py:477
  16.7 34.3 %collective-permute-start = (bf16[3472,128]{1,0:T(8,128)(2,1)}, bf16[3472,128]{1,0:T(8,128)(2,1)S(1)}, u32[]{:S(2)}, u32[]{:S(2)}) collective-permute-start(bf16[3472,128]{1,0:T(8,128)(2,1)} %get-tuple-element.7), channel_id=1, source_target_pairs={{0,127},{1,2},{2,1},{3,4},{4,3},{5,6},{6,5},{7,8},{8,7},{9,10},{10... | collective-permute-start | bytes 2666504 | tf_op jit(solution)/shard_map/ppermute | solution.py:497
  23.0 28.0 %collective-permute-start.1 = (bf16[3472,128]{1,0:T(8,128)(2,1)}, bf16[3472,128]{1,0:T(8,128)(2,1)S(1)}, u32[]{:S(2)}, u32[]{:S(2)}) collective-permute-start(bf16[3472,128]{1,0:T(8,128)(2,1)} %get-tuple-element.8), channel_id=1, source_target_pairs={{0,1},{1,0},{2,3},{3,2},{4,5},{5,4},{6,7},{7,6},{8,9},{9,8},{10,11... | collective-permute-start | bytes 2666504 | tf_op jit(solution)/shard_map/ppermute | solution.py:496
  23.6 0.7 %copy-start.3 = (bf16[64,8,128]{2,1,0:T(8,128)(2,1)}, bf16[64,8,128]{2,1,0:T(8,128)(2,1)S(1)}, u32[]{:S(2)}) copy-start(bf16[64,8,128]{2,1,0:T(8,128)(2,1)S(1)} %all-to-all-done.refs_0_) | copy-start | bytes 393220
  24.3 26.7 %copy-start = (f32[2,16,72,256]{3,2,1,0:T(8,128)S(1)}, f32[2,16,72,256]{3,2,1,0:T(8,128)}, u32[]{:S(2)}) copy-start(f32[2,16,72,256]{3,2,1,0:T(8,128)} %velocity_hbm.3) | copy-start | bytes 7077892
  24.3 26.7 %copy-start.1 = (f32[16,72,256]{2,1,0:T(8,128)S(1)}, f32[16,72,256]{2,1,0:T(8,128)}, u32[]{:S(2)}) copy-start(f32[16,72,256]{2,1,0:T(8,128)} %fields_hbm.3) | copy-start | bytes 3538948
  24.3 26.8 %copy-start.2 = (s32[4,256]{1,0:T(4,128)S(1)}, s32[4,256]{1,0:T(4,128)}, u32[]{:S(2)}) copy-start(s32[4,256]{1,0:T(4,128)} %neighbors_hbm.3) | copy-start | bytes 12292

commit v2 on v1

--- a/solution.py
+++ b/solution.py
@@ -159,7 +159,7 @@
 
 def column_network(*refs):
     operands = refs[:12]
-    out_ref = refs[12]
+    out_hbm = refs[12]
     (
         arrived_ref,
         w_profile_ref,
@@ -173,9 +173,9 @@
         b_third_ref,
         w_out_ref,
         b_out_ref,
-    ) = refs[13:25]
-    table_ref, input_ref, w_first_ref, sems = refs[25:]
-    sources, targets = list(operands), list(refs[13:25])
+    ) = refs[14:26]
+    table_ref, input_ref, w_first_ref, out_ref, sems, out_sems = refs[26:]
+    sources, targets = list(operands), list(refs[14:26])
     sources[4], targets[4] = operands[4].at[0:4], fields_ref.at[0:4]
     sources.append(operands[4].at[4:NODES])
     targets.append(fields_ref.at[4:NODES])
@@ -232,6 +232,7 @@
         copy.wait()
     for j in range(4):
         prepare(j, 0)
+    sent = []
     for block in range(4):
         def ahead(j):
             if block < 3:
@@ -263,6 +264,13 @@
         result = result + b_out
         for j in range(4):
             out_ref[4 * block + j] = result[:, 256 * j : 256 * j + 256].astype(BF16)
+        nodes = slice(4 * block, 4 * block + 4)
+        sent.append(
+            pltpu.make_async_copy(out_ref.at[nodes], out_hbm.at[nodes], out_sems.at[block])
+        )
+        sent[-1].start()
+    for copy in sent:
+        copy.wait()
 
 
 class Dynamics:
@@ -393,7 +401,7 @@
     far_ref,
     near_ref,
     heating_hbm,
-    out_ref,
+    out_hbm,
     same_heating_hbm,
     current_ref,
     velocity_ref,
@@ -402,7 +410,9 @@
     chosen_ref,
     across_ref,
     heating_ref,
+    out_ref,
     sems,
+    out_sems,
 ):
     del same_heating_hbm
     copies = [
@@ -436,8 +446,17 @@
             copies[2].wait()
         dynamics.update(tiles_out)
     copies[3].wait()
-    for n in range(NODES):
-        out_ref[n] = current_ref[n, :, 0:256] + heating_ref[n].astype(F32)
+    sent = []
+    for block in range(4):
+        nodes = slice(4 * block, 4 * block + 4)
+        for n in range(4 * block, 4 * block + 4):
+            out_ref[n] = current_ref[n, :, 0:256] + heating_ref[n].astype(F32)
+        sent.append(
+            pltpu.make_async_copy(out_ref.at[nodes], out_hbm.at[nodes], out_sems.at[block])
+        )
+        sent[-1].start()
+    for copy in sent:
+        copy.wait()
 
 
 def per_device(
@@ -511,17 +530,23 @@
         jnp.transpose(w_out),
         b_out[None, :],
     ]
-    heating = pl.pallas_call(
+    heating, _ = pl.pallas_call(
         column_network,
-        out_shape=jax.ShapeDtypeStruct((NODES, LEV, elem_dev), BF16),
+        out_shape=[
+            jax.ShapeDtypeStruct((NODES, LEV, elem_dev), BF16),
+            jax.ShapeDtypeStruct(arrived.shape, BF16),
+        ],
+        input_output_aliases={0: 1},
         in_specs=[hbm] * len(operands),
-        out_specs=vmem,
+        out_specs=[hbm, hbm],
         scratch_shapes=[pltpu.VMEM(x.shape, x.dtype) for x in operands]
         + [
             pltpu.VMEM((256, 256), BF16),
             pltpu.VMEM((2, 1024, 96), BF16),
             pltpu.VMEM((96, w_second.shape[0]), BF16),
+            pltpu.VMEM((NODES, LEV, elem_dev), BF16),
             pltpu.SemaphoreType.DMA((len(operands) + 1,)),
+            pltpu.SemaphoreType.DMA((4,)),
         ],
         compiler_params=pltpu.CompilerParams(vmem_limit_bytes=NET_LIMIT),
         cost_estimate=pl.CostEstimate(
@@ -537,7 +562,7 @@
         ],
         input_output_aliases={5: 1},
         in_specs=[hbm, hbm, hbm, vmem, vmem, hbm],
-        out_specs=[vmem, hbm],
+        out_specs=[hbm, hbm],
         scratch_shapes=[
             pltpu.VMEM((NODES, LEV, 512), F32),
             pltpu.VMEM(velocity.shape, F32),
@@ -546,6 +571,8 @@
             pltpu.VMEM((4, 512, 512), BF16),
             pltpu.VMEM((4, 4, LEV, 512), F32),
             pltpu.VMEM((NODES, LEV, elem_dev), BF16),
+            pltpu.VMEM((NODES, LEV, elem_dev), F32),
+            pltpu.SemaphoreType.DMA((4,)),
             pltpu.SemaphoreType.DMA((4,)),
         ],
         compiler_params=pltpu.CompilerParams(vmem_limit_bytes=ADVANCE_LIMIT),

time: 60.2 us -> 60.1 us (level)
  no operation moved by 1% of the time
where the time goes in v2:
time: 60.1 us; the launch traced here: 59.1 us
  Pallas kernels  39.1 us (65%)
  starting transfers between devices  17.8 us (30%)
  between operations  0.89 us (1%)
  local copies, waits for them, and re-layouts  0.66 us (1%)
  waiting for transfers between devices  0.62 us (1%)
    pallas_call x1, Pallas kernels, per_device(): pl.pallas_call(column_network, out_shape=[jax.ShapeDtypeStruct((NODES, LE...  26.6 us
    all_to_all x1, starting transfers between devices, per_device(): lax.all_to_all(packed, 'dyn', split_axis=0, concat_axis=0, tiled=True)  11.5 us
    pallas_call x1, Pallas kernels, per_device(): pl.pallas_call(functools.partial(advance, total), out_shape=[jax.ShapeDty...  7.94 us
    ppermute x1, starting transfers between devices, per_device(): lax.ppermute(far, ('dyn', 'grp'), [(i, ((i + 1 ^ 1) - 1) % devices) for i...  6.27 us
    pallas_call x1, Pallas kernels, per_device(): pl.pallas_call(functools.partial(pack_halo, total), out_shape=[jax.ShapeD...  2.88 us
    pallas_call x1, Pallas kernels, per_device(): pl.pallas_call(pack_surface, out_shape=[jax.ShapeDtypeStruct((chips, 8, L...  1.68 us
  transfers between devices with their start and end apart: 3, of which 1 were waited for; matrix products, arithmetic and copies ran while one was open for 0% of the time, Pallas kernels for 50%

profile of v2, /device:TPU:0, one launch (start us, length us, event | category | flops | bytes accessed | tf_op | source)
XLA Modules:
  0.0 59.1 jit_solution(18213080654075966558)
XLA Ops:
  0.6 1.7 %pack_surface.1 = (bf16[64,8,128]{2,1,0:T(8,128)(2,1)}, f32[8,128]{1,0:T(8,128)}) custom-call(bf16[16,8192]{1,0:T(8,128)(2,1)} %surface_ref.1), custom_call_target="tpu_custom_call" | custom-call | tf_op jit(solution)/shard_map/pack_surface/pallas_call | solution.py:485
  2.3 11.5 %all-to-all-start = ((bf16[64,8,128]{2,1,0:T(8,128)(2,1)}), bf16[64,8,128]{2,1,0:T(8,128)(2,1)S(1)}, u32[]{:S(2)}, u32[]{:S(2)}) async-start(bf16[64,8,128]{2,1,0:T(8,128)(2,1)} %get-tuple-element.10), calls=%async_computation | async-start | bytes 262144 | tf_op jit(solution)/shard_map/all_to_all | solution.py:496
  13.8 2.9 %pack_halo.1 = (bf16[3472,128]{1,0:T(8,128)(2,1)}, bf16[3472,128]{1,0:T(8,128)(2,1)}) custom-call(f32[8,128]{1,0:T(8,128)} %get-tuple-element.7.token_ref, f32[16,72,256]{2,1,0:T(8,128)} %fields_hbm.3, f32[2,16,72,256]{3,2,1,0:T(8,128)} %velocity_hbm.3, s32[4,256]{1,0:T(4,128)} %neighbors_hbm.3), custom_call_target="tpu_custom_call" | custom-call | flops 1000000 | bytes 7000000 | tf_op jit(solution)/shard_map/pack_halo/pallas_call | solution.py:497
  16.7 6.3 %collective-permute-start = (bf16[3472,128]{1,0:T(8,128)(2,1)}, bf16[3472,128]{1,0:T(8,128)(2,1)S(1)}, u32[]{:S(2)}, u32[]{:S(2)}) collective-permute-start(bf16[3472,128]{1,0:T(8,128)(2,1)} %get-tuple-element.8), channel_id=1, source_target_pairs={{0,127},{1,2},{2,1},{3,4},{4,3},{5,6},{6,5},{7,8},{8,7},{9,10},{10... | collective-permute-start | bytes 2666504 | tf_op jit(solution)/shard_map/ppermute | solution.py:516
  23.0 0.0 collective-permute-start.1
  23.0 0.6 %all-to-all-done.refs_0_ = bf16[64,8,128]{2,1,0:T(8,128)(2,1)S(1)} async-done(((bf16[64,8,128]{2,1,0:T(8,128)(2,1)}), bf16[64,8,128]{2,1,0:T(8,128)(2,1)S(1)}, u32[]{:S(2)}, u32[]{:S(2)}) %all-to-all-start) | async-done | bytes 131104 | tf_op jit(solution)/shard_map/all_to_all | solution.py:496
  23.6 0.0 copy-start.3
  23.6 0.6 %copy-done.3 = bf16[64,8,128]{2,1,0:T(8,128)(2,1)} copy-done((bf16[64,8,128]{2,1,0:T(8,128)(2,1)}, bf16[64,8,128]{2,1,0:T(8,128)(2,1)S(1)}, u32[]{:S(2)}) %copy-start.3) | copy-done | bytes 131096
  24.3 0.0 copy-start
  24.3 0.0 copy-start.1
  24.3 0.0 copy-start.2
  24.3 26.6 %column_network.1 = (bf16[16,72,256]{2,1,0:T(8,128)(2,1)}, bf16[64,8,128]{2,1,0:T(8,128)(2,1)}) custom-call(bf16[64,8,128]{2,1,0:T(8,128)(2,1)} %copy-done.3, bf16[72,1024]{1,0:T(8,128)(2,1)} %refs_1_.1, bf16[16,1024]{1,0:T(8,128)(2,1)} %refs_2_.1, s32[16,256]{1,0:T(8,128)} %refs_3_.1, f32[16,72,256]{2,1,0:T(8,128)} %fields_hbm.3, ...), custom_call_target="tpu_custom_call", output_to_operand_aliasing={{1}: (0, {})} | custom-call | flops 22000001024 | bytes 8000000 | tf_op jit(solution)/shard_map/column_network/pallas_call | solution.py:533
  50.9 0.0 collective-permute-done.far_ref
  50.9 0.0 collective-permute-done.1.near_ref
  50.9 0.0 copy-done
  50.9 0.0 copy-done.1
  50.9 0.0 copy-done.2
  50.9 7.9 %advance.1 = (f32[16,72,256]{2,1,0:T(8,128)}, bf16[16,72,256]{2,1,0:T(8,128)(2,1)}) custom-call(f32[16,72,256]{2,1,0:T(8,128)S(1)} %copy-done.1, f32[2,16,72,256]{3,2,1,0:T(8,128)S(1)} %copy-done, s32[4,256]{1,0:T(4,128)S(1)} %copy-done.2, bf16[3472,128]{1,0:T(8,128)(2,1)S(1)} %collective-permute-done.far_ref, ...), custom_call_target="tpu_custom_call", output_to_operand_aliasing={{1}: (5, {})} | custom-call | flops 2000000000 | bytes 10000000 | tf_op jit(solution)/shard_map/advance/pallas_call | solution.py:557
Async XLA Ops:
  2.3 21.3 %all-to-all-start = ((bf16[64,8,128]{2,1,0:T(8,128)(2,1)}), bf16[64,8,128]{2,1,0:T(8,128)(2,1)S(1)}, u32[]{:S(2)}, u32[]{:S(2)}) async-start(bf16[64,8,128]{2,1,0:T(8,128)(2,1)} %get-tuple-element.10), calls=%async_computation | async-start | bytes 262144 | tf_op jit(solution)/shard_map/all_to_all | solution.py:496
  16.7 34.2 %collective-permute-start = (bf16[3472,128]{1,0:T(8,128)(2,1)}, bf16[3472,128]{1,0:T(8,128)(2,1)S(1)}, u32[]{:S(2)}, u32[]{:S(2)}) collective-permute-start(bf16[3472,128]{1,0:T(8,128)(2,1)} %get-tuple-element.8), channel_id=1, source_target_pairs={{0,127},{1,2},{2,1},{3,4},{4,3},{5,6},{6,5},{7,8},{8,7},{9,10},{10... | collective-permute-start | bytes 2666504 | tf_op jit(solution)/shard_map/ppermute | solution.py:516
  23.0 27.9 %collective-permute-start.1 = (bf16[3472,128]{1,0:T(8,128)(2,1)}, bf16[3472,128]{1,0:T(8,128)(2,1)S(1)}, u32[]{:S(2)}, u32[]{:S(2)}) collective-permute-start(bf16[3472,128]{1,0:T(8,128)(2,1)} %get-tuple-element.9), channel_id=1, source_target_pairs={{0,1},{1,0},{2,3},{3,2},{4,5},{5,4},{6,7},{7,6},{8,9},{9,8},{10,11... | collective-permute-start | bytes 2666504 | tf_op jit(solution)/shard_map/ppermute | solution.py:515
  23.6 0.6 %copy-start.3 = (bf16[64,8,128]{2,1,0:T(8,128)(2,1)}, bf16[64,8,128]{2,1,0:T(8,128)(2,1)S(1)}, u32[]{:S(2)}) copy-start(bf16[64,8,128]{2,1,0:T(8,128)(2,1)S(1)} %all-to-all-done.refs_0_) | copy-start | bytes 393220
  24.3 26.6 %copy-start = (f32[2,16,72,256]{3,2,1,0:T(8,128)S(1)}, f32[2,16,72,256]{3,2,1,0:T(8,128)}, u32[]{:S(2)}) copy-start(f32[2,16,72,256]{3,2,1,0:T(8,128)} %velocity_hbm.3) | copy-start | bytes 7077892
  24.3 26.6 %copy-start.1 = (f32[16,72,256]{2,1,0:T(8,128)S(1)}, f32[16,72,256]{2,1,0:T(8,128)}, u32[]{:S(2)}) copy-start(f32[16,72,256]{2,1,0:T(8,128)} %fields_hbm.3) | copy-start | bytes 3538948
  24.3 26.7 %copy-start.2 = (s32[4,256]{1,0:T(4,128)S(1)}, s32[4,256]{1,0:T(4,128)}, u32[]{:S(2)}) copy-start(s32[4,256]{1,0:T(4,128)} %neighbors_hbm.3) | copy-start | bytes 12292
